TPU v7x, 256 devices: a whole 4x4x8 slice. The times are simulated.
256 devices in a mesh: pipe: 16 (over y, x_lo, core), fsdp: 8 (over z), tp: 2 (over x_hi).
Axes of the slice: x: 4 (x_hi: 2, x_lo: 2; x = x_hi * 2 + x_lo), y: 4, z: 8, core: 2. Of those that a mesh axis runs over, the one named last changes fastest.
Arguments:
- act_in: bfloat16 [16, 2, 8, 128, 4096], P('pipe', None, 'fsdp', None, 'tp'), may hold values from -6 to 6
- gate_q: bfloat16 [16, 2, 8, 128, 4096], P('pipe', None, 'fsdp', None, 'tp'), may hold values from -6 to 6
- gate_k: bfloat16 [16, 2, 8, 128, 4096], P('pipe', None, 'fsdp', None, 'tp'), may hold values from -6 to 6
- grad_in: bfloat16 [16, 8, 128, 4096], P('pipe', 'fsdp', None, 'tp'), may hold values from -6 to 6
- weight: bfloat16 [16, 4096, 4096], P('pipe', 'tp', 'fsdp'), may hold values from -0.09375 to 0.09375
- filters: bfloat16 [16, 128, 256], P('pipe', None, 'tp'), may hold values from -0.5 to 0.5
Outputs:
- grad_out: bfloat16 [16, 2, 8, 128, 4096], P('pipe', None, 'fsdp', None, 'tp')
- filter_grad: float32 [16, 128, 256], P('pipe', 'fsdp', 'tp')
All inputs are finite; a program needn't handle non-finite values.
Results may differ from a plain program's by a relative error of at most 0.0056.
Values may be sent and summed in bfloat16 or wider, within the bound.
No kernel may reach another device: no remote copies, remote signals or barrier semaphores. Data moves between devices by JAX's collectives and lax.ppermute only.
A program may use at most 128 MiB of HBM per device.

v0:
```python
import math
import jax
import jax.numpy as jnp
from jax import lax
from jax.sharding import PartitionSpec as P


def passed_along(value, axis, by):
    peers = lax.axis_size(axis)
    pairs = [(i, i + by) for i in range(peers) if 0 <= i + by < peers]
    return lax.ppermute(value, axis, pairs)


def toeplitz(taps_table, seqlen):
    rows = taps_table.T
    padded = jnp.pad(rows, ((0, 0), (0, 2 * seqlen - rows.shape[1])))
    tiled = jnp.tile(padded, (1, seqlen))
    cut = tiled[:, : seqlen * (2 * seqlen - 1)].reshape(rows.shape[0], seqlen, 2 * seqlen - 1)
    return cut[:, :, :seqlen]


def filter_terms(adjoint, shaped, taps):
    seqlen = adjoint.shape[0]
    groups_loc = adjoint.shape[1]
    flipped = jnp.pad(shaped[::-1], ((0, taps), (0, 0), (0, 0)))
    span = seqlen + taps
    block = math.gcd(groups_loc, 16)
    pieces = []
    for first in range(0, groups_loc, block):
        corr = jnp.einsum(
            "tgc,ugc->gtu",
            adjoint[:, first : first + block],
            flipped[:, first : first + block],
            preferred_element_type=jnp.float32,
        )
        flat = corr.reshape(block, seqlen * span)[:, : seqlen * (span - 1)]
        skewed = flat.reshape(block, seqlen, span - 1)[:, :, seqlen - 1 : seqlen - 1 + taps]
        pieces.append(jnp.sum(skewed, axis=1))
    return jnp.concatenate(pieces, axis=0).T


def body(act_in, gate_q, gate_k, grad_in, weight, filters):
    ticks = act_in.shape[1]
    seqlen = act_in.shape[3]
    width_loc = act_in.shape[4]
    taps = filters.shape[1]
    groups_loc = filters.shape[2]
    per_group = width_loc // groups_loc
    scale = 1.0 / math.sqrt(ticks * lax.axis_size("fsdp") * seqlen * per_group)
    kernel = toeplitz(filters[0], seqlen)
    contract = (((1,), (1,)), ((), ()))
    incoming = grad_in[0, 0]
    outputs = []
    pending = jnp.zeros((taps, groups_loc), jnp.float32)
    for tick in range(ticks):
        if tick > 0:
            incoming = passed_along(outputs[-1], "pipe", -1)
        whole = lax.all_gather(incoming, "tp", axis=1, tiled=True)

        def add_panel(total, piece, start, whole=whole):
            return lax.dot_general(whole, piece, contract, preferred_element_type=jnp.float32)

        deriv = add_panel(
            jnp.zeros((seqlen, width_loc), jnp.float32),
            lax.all_gather(weight[0], "fsdp", axis=1, tiled=True),
            jnp.int32(0),
        )
        adjoint = (
            (gate_q[0, tick, 0] * deriv).astype(jnp.bfloat16).reshape(seqlen, groups_loc, per_group)
        )
        back = jnp.einsum(
            "gtu,ugc->tgc", kernel, adjoint, preferred_element_type=jnp.float32
        ).reshape(seqlen, width_loc)
        result = (incoming + gate_k[0, tick, 0] * back).astype(jnp.bfloat16)
        outputs.append(result)
        shaped = (
            gate_k[0, tick, 0].astype(jnp.float32) * act_in[0, tick, 0].astype(jnp.float32)
        ).astype(jnp.bfloat16)
        term = filter_terms(adjoint, shaped.reshape(seqlen, groups_loc, per_group), taps) * scale
        pending = pending + term
    summed = lax.psum_scatter(pending, "fsdp", scatter_dimension=0, tiled=True)
    grads = jnp.stack(outputs, axis=0)[None, :, None]
    return (grads, summed[None])


def solution(mesh):
    placed = (
        P("pipe", None, "fsdp", None, "tp"),
        P("pipe", None, "fsdp", None, "tp"),
        P("pipe", None, "fsdp", None, "tp"),
        P("pipe", "fsdp", None, "tp"),
        P("pipe", "tp", "fsdp"),
        P("pipe", None, "tp"),
    )
    return jax.shard_map(
        body,
        mesh=mesh,
        in_specs=placed,
        out_specs=(P("pipe", None, "fsdp", None, "tp"), P("pipe", "fsdp", "tp")),
        check_vma=False,
    )
```

profile of v0, /device:TPU:2, one launch (start us, length us, event | category | flops | bytes accessed | tf_op | source)
XLA Modules:
  0.0 514.4 jit_solution(2104143820232488051)
XLA Ops:
  8.9 3.8 tile.4
  12.7 12.3 %copy.61 = bf16[16,8,128,256]{3,1,2,0:T(8,128)(2,1)} copy(bf16[16,8,128,256]{3,2,1,0:T(8,128)(2,1)} %bitcast.136) | data formatting | bytes 16777216
  25.0 7.4 %slice.290 = bf16[128,32640]{1,0:T(8,128)(2,1)} slice(bf16[128,32768]{1,0:T(8,128)(2,1)} %bitcast.137), slice={[0:128], [0:32640]} | slice | bytes 16711680 | tf_op jit(solution)/shard_map/slice | solution.py:18
  32.4 29.8 %reshape.184 = bf16[128,128,255]{2,1,0:T(8,128)(2,1)} reshape(bf16[128,32640]{1,0:T(8,128)(2,1)} %slice.290) | data formatting | bytes 16711680 | tf_op jit(solution)/shard_map/reshape | solution.py:18
  64.0 150.7 %all-gather.10.cloned.1.call-done = bf16[1,2048,4096]{2,1,0:T(8,128)(2,1)} async-done(((bf16[1,2048,512]{2,1,0:T(8,128)(2,1)}), bf16[1,2048,4096]{2,1,0:T(8,128)(2,1)}) %all-gather.10.cloned.1.call-update) | async-done | bytes 16777232 | tf_op jit(solution)/shard_map/all_gather | solution.py:65
  214.7 11.8 %fusion.17 = bf16[128,2048]{1,0:T(8,128)(2,1)S(1)} fusion(bf16[1,2048,4096]{2,1,0:T(8,128)(2,1)} %all-gather.10.cloned.1.call-done, bf16[1,1,128,4096]{3,2,1,0:T(8,128)(2,1)} %all-gather.8.cloned.1.call-done, bf16[1,2,1,128,2048]{4,3,2,1,0:T(8,128)(2,1)S(1)} %copy-done.9), kind=kOutput, calls=%fused_computation.11 | convolution fusion | flops 2148270080 | bytes 18874368 | tf_op jit(solution)/shard_map/dot_general | solution.py:61
  247.9 6.2 %reshape.190 = f32[16,128,255]{2,1,0:T(8,128)} reshape(f32[16,32640]{1,0:T(8,128)} %slice.292) | data formatting | bytes 4177920 | tf_op jit(solution)/shard_map/reshape | solution.py:37
  256.1 2.8 copy.63
  260.4 6.1 %reshape.192 = f32[16,128,255]{2,1,0:T(8,128)} reshape(f32[16,32640]{1,0:T(8,128)} %slice.294) | data formatting | bytes 4177920 | tf_op jit(solution)/shard_map/reshape | solution.py:37
  272.7 6.1 %reshape.194 = f32[16,128,255]{2,1,0:T(8,128)} reshape(f32[16,32640]{1,0:T(8,128)} %slice.296) | data formatting | bytes 4177920 | tf_op jit(solution)/shard_map/reshape | solution.py:37
  280.8 3.2 copy.65
  285.5 6.1 %reshape.196 = f32[16,128,255]{2,1,0:T(8,128)} reshape(f32[16,32640]{1,0:T(8,128)} %slice.298) | data formatting | bytes 4177920 | tf_op jit(solution)/shard_map/reshape | solution.py:37
  297.8 6.3 %reshape.198 = f32[16,128,255]{2,1,0:T(8,128)} reshape(f32[16,32640]{1,0:T(8,128)} %slice.300) | data formatting | bytes 4177920 | tf_op jit(solution)/shard_map/reshape | solution.py:37
  310.3 6.1 %reshape.200 = f32[16,128,255]{2,1,0:T(8,128)} reshape(f32[16,32640]{1,0:T(8,128)} %slice.302) | data formatting | bytes 4177920 | tf_op jit(solution)/shard_map/reshape | solution.py:37
  326.3 6.2 %reshape.202 = f32[16,128,255]{2,1,0:T(8,128)} reshape(f32[16,32640]{1,0:T(8,128)} %slice.304) | data formatting | bytes 4177920 | tf_op jit(solution)/shard_map/reshape | solution.py:37
  332.5 3.0 copy.69
  336.9 6.1 %reshape.204 = f32[16,128,255]{2,1,0:T(8,128)} reshape(f32[16,32640]{1,0:T(8,128)} %slice.306) | data formatting | bytes 4177920 | tf_op jit(solution)/shard_map/reshape | solution.py:37
  349.5 12.0 %fusion.14 = bf16[128,2048]{1,0:T(8,128)(2,1)S(1)} fusion(bf16[128,4096]{1,0:T(8,128)(2,1)} %all-gather.6.cloned.1.call-done, bf16[1,2048,4096]{2,1,0:T(8,128)(2,1)} %all-gather.10.cloned.1.call-done, bf16[1,2,1,128,2048]{4,3,2,1,0:T(8,128)(2,1)} %param.7), kind=kOutput, calls=%fused_computation.10 | convolution fusion | flops 2148270080 | bytes 18874368 | tf_op jit(solution)/shard_map/dot_general | solution.py:61
  372.6 3.3 fusion.4
  378.6 6.2 %reshape.206 = f32[16,128,255]{2,1,0:T(8,128)} reshape(f32[16,32640]{1,0:T(8,128)} %slice.308) | data formatting | bytes 4177920 | tf_op jit(solution)/shard_map/reshape | solution.py:37
  386.8 2.8 copy.71
  391.1 6.1 %reshape.208 = f32[16,128,255]{2,1,0:T(8,128)} reshape(f32[16,32640]{1,0:T(8,128)} %slice.310) | data formatting | bytes 4177920 | tf_op jit(solution)/shard_map/reshape | solution.py:37
  399.2 3.2 copy.72
  403.8 6.2 %reshape.210 = f32[16,128,255]{2,1,0:T(8,128)} reshape(f32[16,32640]{1,0:T(8,128)} %slice.312) | data formatting | bytes 4177920 | tf_op jit(solution)/shard_map/reshape | solution.py:37
  411.9 2.8 copy.73
  416.2 6.2 %reshape.212 = f32[16,128,255]{2,1,0:T(8,128)} reshape(f32[16,32640]{1,0:T(8,128)} %slice.314) | data formatting | bytes 4177920 | tf_op jit(solution)/shard_map/reshape | solution.py:37
  428.6 6.2 %reshape.214 = f32[16,128,255]{2,1,0:T(8,128)} reshape(f32[16,32640]{1,0:T(8,128)} %slice.316) | data formatting | bytes 4177920 | tf_op jit(solution)/shard_map/reshape | solution.py:37
  436.7 3.0 copy.75
  441.1 6.2 %reshape.216 = f32[16,128,255]{2,1,0:T(8,128)} reshape(f32[16,32640]{1,0:T(8,128)} %slice.318) | data formatting | bytes 4177920 | tf_op jit(solution)/shard_map/reshape | solution.py:37
  453.5 6.2 %reshape.218 = f32[16,128,255]{2,1,0:T(8,128)} reshape(f32[16,32640]{1,0:T(8,128)} %slice.320) | data formatting | bytes 4177920 | tf_op jit(solution)/shard_map/reshape | solution.py:37
  463.0 4.6 reshape.220
  473.2 32.9 %reduce-scatter.4.cloned.1.call-done = f32[16,128]{1,0:T(8,128)} async-done(((f32[128,128]{1,0:T(8,128)}), f32[16,128]{1,0:T(8,128)}) %reduce-scatter.4.cloned.1.call-update) | async-done | bytes 8208
  (137 shorter events, 117.9 us)
Async XLA Ops:
  7.2 1.5 copy-start.10
  7.2 56.8 %all-gather.8.cloned.1.call-start = ((), (), s32[]{:S(2)}) async-start(), calls=%async_computation.2 | async-start | bytes 1572864 | tf_op jit(solution)/shard_map/all_gather | solution.py:58
  7.9 206.8 %all-gather.10.cloned.1.call-start = ((), (), s32[]{:S(2)}) async-start(), calls=%async_computation.3 | async-start | bytes 18874368 | tf_op jit(solution)/shard_map/all_gather | solution.py:65
  8.7 340.8 %all-gather.6.cloned.1.call-start = ((), (), s32[]{:S(2)}) async-start(), calls=%async_computation.1 | async-start | bytes 1572864 | tf_op jit(solution)/shard_map/all_gather | solution.py:58
  32.4 29.8 %copy-start.1 = (bf16[1,2,1,128,2048]{4,3,2,1,0:T(8,128)(2,1)S(1)}, bf16[1,2,1,128,2048]{4,3,2,1,0:T(8,128)(2,1)}, u32[]{:S(2)}) copy-start(bf16[1,2,1,128,2048]{4,3,2,1,0:T(8,128)(2,1)} %param.8) | copy-start | bytes 3145732
  32.4 29.8 %copy-start.8 = (bf16[1,2,1,128,2048]{4,3,2,1,0:T(8,128)(2,1)S(1)}, bf16[1,2,1,128,2048]{4,3,2,1,0:T(8,128)(2,1)}, u32[]{:S(2)}) copy-start(bf16[1,2,1,128,2048]{4,3,2,1,0:T(8,128)(2,1)} %param.6) | copy-start | bytes 3145732
  62.6 152.1 %copy-start.9 = (bf16[1,2,1,128,2048]{4,3,2,1,0:T(8,128)(2,1)S(1)}, bf16[1,2,1,128,2048]{4,3,2,1,0:T(8,128)(2,1)}, u32[]{:S(2)}) copy-start(bf16[1,2,1,128,2048]{4,3,2,1,0:T(8,128)(2,1)} %param.7) | copy-start | bytes 3145732
  226.8 10.2 %slice-start = ((s8[8388608]{0:T(1024)(128)(4,1)}), s8[4194304]{0:T(1024)(128)(4,1)S(1)}, s32[]{:S(2)}) async-start(s8[8388608]{0:T(1024)(128)(4,1)} %bitcast.132), calls=%async_computation.5 | async-start | bytes 8388608
  231.8 5.1 slice-start.1
  239.2 1.3 copy-start.4
  240.5 4.7 copy-start
  243.1 78.7 %collective-permute-start = (bf16[128,2048]{1,0:T(8,128)(2,1)}, bf16[128,2048]{1,0:T(8,128)(2,1)}, u32[]{:S(2)}, u32[]{:S(2)}) collective-permute-start(bf16[128,2048]{1,0:T(8,128)(2,1)} %fusion.23), channel_id=1, source_target_pairs={{16,0},{32,16},{48,32},{64,48},{80,64},{96,80},{112,96},{128,112},... | collective-permute-start | bytes 1572872 | tf_op jit(solution)/shard_map/ppermute | solution.py:11
  321.8 184.3 %reduce-scatter.4.cloned.1.call-start = ((), (), s32[]{:S(2)}) async-start(), calls=%async_computation.4 | async-start | bytes 73728
  343.1 5.3 %copy-start.2 = (bf16[1,2,1,128,2048]{4,3,2,1,0:T(8,128)(2,1)S(1)}, bf16[1,2,1,128,2048]{4,3,2,1,0:T(8,128)(2,1)}, u32[]{:S(2)}) copy-start(bf16[1,2,1,128,2048]{4,3,2,1,0:T(8,128)(2,1)} %param.8) | copy-start | bytes 3145732
  344.4 4.0 copy-start.5
  363.7 8.8 %slice-start.2 = ((s8[8388608]{0:T(1024)(128)(4,1)}), s8[4194304]{0:T(1024)(128)(4,1)S(1)}, s32[]{:S(2)}) async-start(s8[8388608]{0:T(1024)(128)(4,1)} %bitcast.134), calls=%async_computation.7 | async-start | bytes 8388608
  368.8 3.8 slice-start.3
  463.0 7.5 %copy-start.6 = (f32[128,16,128]{2,1,0:T(8,128)S(1)}, f32[128,16,128]{2,1,0:T(8,128)}, u32[]{:S(2)}) copy-start(f32[128,16,128]{2,1,0:T(8,128)} %fusion.4) | copy-start | bytes 3145732
  467.6 3.2 copy-start.3
  470.8 1.3 copy-start.7
Sparse Core Ops, SparseCore 0:
  9.8 29.9 all-gather.7
  41.6 173.1 all-gather.9
  322.0 26.2 all-gather.5
  470.6 35.5 reduce-scatter.3
where the time goes:
time: 522 us; the launch traced here: 514 us
  local copies, waits for them, and re-layouts  221 us (42%)
  waiting for transfers between devices  185 us (35%)
  matrix products  53.6 us (10%)
  other arithmetic  37.5 us (7%)
  between operations  14.5 us (3%)
    all_gather x1, waiting for transfers between devices, body(): lax.all_gather(weight[0], 'fsdp', axis=1, tiled=True)  151 us
    reshape x16, local copies, waits for them, and re-layouts, filter_terms(): flat.reshape(block, seqlen, span - 1)[:, :, seqlen - 1:seqlen - 1 + taps]  97.1 us
    unnamed x65, local copies, waits for them, and re-layouts  56 us
    unnamed x5, waiting for transfers between devices  34.4 us
    reduce_sum x16, other arithmetic, filter_terms(): pieces.append(jnp.sum(skewed, axis=1))  31.1 us
    reshape x1, local copies, waits for them, and re-layouts, toeplitz(): tiled[:, :seqlen * (2 * seqlen - 1)]  29.8 us
    dot_general x16, matrix products, filter_terms(): jnp.einsum('tgc,ugc->gtu', adjoint[:, first:first + block], flipped[:, fi...  24.3 us
    dot_general x2, matrix products, add_panel(): lax.dot_general(whole, piece, contract, preferred_element_type=jnp.float32)  23.7 us
  transfers between devices with their start and end apart: 5, of which 2 were waited for; matrix products, arithmetic and copies ran while one was open for 31% of the time, Pallas kernels for 0%

commit v1 on v0

--- a/solution.py
+++ b/solution.py
@@ -3,6 +3,28 @@
 import jax.numpy as jnp
 from jax import lax
 from jax.sharding import PartitionSpec as P
+
+
+def laid_out(blocks, dim):
+    shape = list(blocks.shape[1:])
+    shape[dim] *= blocks.shape[0]
+    return jnp.moveaxis(blocks, 0, dim).reshape(shape)
+
+
+def collect(x, axis, dim):
+    size = lax.axis_size(axis)
+    pairs = [(i, (i + 1) % size) for i in range(size)]
+    back = [(b, a) for a, b in pairs]
+    lower, upper = ([], [])
+    for step in range(size - 1):
+        if step % 2 == 0:
+            lower.append(lax.ppermute(lower[-1] if lower else x, axis, pairs))
+        else:
+            upper.append(lax.ppermute(upper[-1] if upper else x, axis, back))
+    blocks = jnp.stack([*lower[::-1], x, *upper])
+    shift = lax.axis_index(axis) - len(lower)
+    blocks = blocks[(jnp.arange(size) - shift) % size]
+    return laid_out(blocks, dim)
 
 
 def passed_along(value, axis, by):
@@ -61,9 +83,7 @@
             return lax.dot_general(whole, piece, contract, preferred_element_type=jnp.float32)
 
         deriv = add_panel(
-            jnp.zeros((seqlen, width_loc), jnp.float32),
-            lax.all_gather(weight[0], "fsdp", axis=1, tiled=True),
-            jnp.int32(0),
+            jnp.zeros((seqlen, width_loc), jnp.float32), collect(weight[0], "fsdp", 1), jnp.int32(0)
         )
         adjoint = (
             (gate_q[0, tick, 0] * deriv).astype(jnp.bfloat16).reshape(seqlen, groups_loc, per_group)

time: 522 us -> 625 us (1.20)
  local copies, waits for them, and re-layouts: 221 us -> 281 us
  waiting for transfers between devices: 185 us -> 206 us
  other arithmetic: 37.5 us -> 53.1 us
  starting transfers between devices: 2.45 us -> 15 us
    ppermute x0 -> x7, waiting for transfers between devices: none -> 172 us  [the longest x4 139 us: collect(): lower.append(lax.ppermute(lower[-1] if lower else x, axis, pairs))]
    all_gather x1 -> x0, waiting for transfers between devices: 151 us -> none  [body(): lax.all_gather(weight[0], 'fsdp', axis=1, tiled=True)]
    gather x0 -> x3, local copies, waits for them, and re-layouts: none -> 22.1 us  [collect(): blocks = blocks[(jnp.arange(size) - shift) % size]]
    transpose x0 -> x1, local copies, waits for them, and re-layouts: none -> 21.6 us  [laid_out(): return jnp.moveaxis(blocks, 0, dim).reshape(shape)]
    transpose x0 -> x1, other arithmetic: none -> 13.6 us  [laid_out(): return jnp.moveaxis(blocks, 0, dim).reshape(shape)]
    ppermute x0 -> x7, starting transfers between devices: none -> 12.2 us  [the longest x3 10.2 us: collect(): upper.append(lax.ppermute(upper[-1] if upper else x, axis, back))]
    unnamed x65 -> x81, local copies, waits for them, and re-layouts: 56 us -> 67.6 us
    unnamed x5 -> x4, waiting for transfers between devices: 34.4 us -> 34 us
  transfers between devices with their start and end apart: 5 -> 11, of which waited for: 2 -> 5; matrix products, arithmetic and copies ran while one was open for 31% -> 38% of each run, Pallas kernels for 0% -> 0%
where the time goes in v1:
time: 625 us; the launch traced here: 619 us
  local copies, waits for them, and re-layouts  281 us (45%)
  waiting for transfers between devices  206 us (33%)
  other arithmetic  53.1 us (8%)
  matrix products  49.2 us (8%)
  starting transfers between devices  15 us (2%)
  between operations  14.8 us (2%)
    ppermute x4, waiting for transfers between devices, collect(): lower.append(lax.ppermute(lower[-1] if lower else x, axis, pairs))  139 us
    reshape x16, local copies, waits for them, and re-layouts, filter_terms(): flat.reshape(block, seqlen, span - 1)[:, :, seqlen - 1:seqlen - 1 + taps]  97.5 us
    unnamed x81, local copies, waits for them, and re-layouts  67.6 us
    unnamed x4, waiting for transfers between devices  34 us
    ppermute x3, waiting for transfers between devices, collect(): upper.append(lax.ppermute(upper[-1] if upper else x, axis, back))  33.2 us
    reduce_sum x16, other arithmetic, filter_terms(): pieces.append(jnp.sum(skewed, axis=1))  31.1 us
    reshape x1, local copies, waits for them, and re-layouts, toeplitz(): tiled[:, :seqlen * (2 * seqlen - 1)]  29.5 us
    dot_general x16, matrix products, filter_terms(): jnp.einsum('tgc,ugc->gtu', adjoint[:, first:first + block], flipped[:, fi...  24.5 us
  transfers between devices with their start and end apart: 11, of which 5 were waited for; matrix products, arithmetic and copies ran while one was open for 38% of the time, Pallas kernels for 0%

profile of v1, /device:TPU:2, one launch (start us, length us, event | category | flops | bytes accessed | tf_op | source)
XLA Modules:
  0.0 618.8 jit_solution(3314686142730985370)
XLA Ops:
  9.2 49.8 %collective-permute-done = bf16[2048,512]{1,0:T(8,128)(2,1)S(1)} collective-permute-done((bf16[2048,512]{1,0:T(8,128)(2,1)}, bf16[2048,512]{1,0:T(8,128)(2,1)S(1)}, u32[]{:S(2)}, u32[]{:S(2)}) %collective-permute-start) | collective-permute-done | bytes 2097184 | tf_op jit(solution)/shard_map/ppermute | solution.py:21
  62.2 44.8 %collective-permute-done.1 = bf16[2048,512]{1,0:T(8,128)(2,1)S(1)} collective-permute-done((bf16[2048,512]{1,0:T(8,128)(2,1)S(1)}, bf16[2048,512]{1,0:T(8,128)(2,1)S(1)}, u32[]{:S(2)}, u32[]{:S(2)}) %collective-permute-start.1) | collective-permute-done | bytes 2097184 | tf_op jit(solution)/shard_map/ppermute | solution.py:21
  111.6 44.0 %collective-permute-done.2 = bf16[2048,512]{1,0:T(8,128)(2,1)} collective-permute-done((bf16[2048,512]{1,0:T(8,128)(2,1)S(1)}, bf16[2048,512]{1,0:T(8,128)(2,1)}, u32[]{:S(2)}, u32[]{:S(2)}) %collective-permute-start.2) | collective-permute-done | bytes 2097184 | tf_op jit(solution)/shard_map/ppermute | solution.py:21
  158.0 3.8 tile.4
  161.8 12.3 %copy.65 = bf16[16,8,128,256]{3,1,2,0:T(8,128)(2,1)} copy(bf16[16,8,128,256]{3,2,1,0:T(8,128)(2,1)} %bitcast.153) | data formatting | bytes 16777216
  174.2 7.1 %slice.294 = bf16[128,32640]{1,0:T(8,128)(2,1)} slice(bf16[128,32768]{1,0:T(8,128)(2,1)} %bitcast.154), slice={[0:128], [0:32640]} | slice | bytes 16711680 | tf_op jit(solution)/shard_map/slice | solution.py:40
  181.3 29.5 %reshape.238 = bf16[128,128,255]{2,1,0:T(8,128)(2,1)} reshape(bf16[128,32640]{1,0:T(8,128)(2,1)} %slice.294) | data formatting | bytes 16711680 | tf_op jit(solution)/shard_map/reshape | solution.py:40
  231.6 33.2 %collective-permute-done.6 = bf16[2048,512]{1,0:T(8,128)(2,1)S(1)} collective-permute-done((bf16[2048,512]{1,0:T(8,128)(2,1)}, bf16[2048,512]{1,0:T(8,128)(2,1)S(1)}, u32[]{:S(2)}, u32[]{:S(2)}) %collective-permute-start.6) | collective-permute-done | bytes 2097184 | tf_op jit(solution)/shard_map/ppermute | solution.py:23
  264.9 6.0 fusion.54
  270.9 8.1 %gather_fusion = bf16[8,1024,512]{2,1,0:T(8,128)(2,1)} fusion(bf16[8,1024,512]{2,1,0:T(8,128)(2,1)} %get-tuple-element.6, s32[1024]{0:T(1024)S(1)} %pad_clamp_fusion), kind=kCustom, calls=%fused_computation | custom fusion | bytes 16777248 | tf_op jit(solution)/shard_map/gather | solution.py:26
  279.0 8.0 %gather_fusion.1 = bf16[8,1024,512]{2,1,0:T(8,128)(2,1)} fusion(bf16[8,1024,512]{2,1,0:T(8,128)(2,1)} %get-tuple-element.7, s32[1024]{0:T(1024)S(1)} %pad_clamp_fusion), kind=kCustom, calls=%fused_computation.1 | custom fusion | bytes 16777248 | tf_op jit(solution)/shard_map/gather | solution.py:26
  287.0 13.6 %maximum_bitcast_fusion = bf16[2048,8,512]{2,0,1:T(8,128)(2,1)} fusion(bf16[8,1024,512]{2,1,0:T(8,128)(2,1)} %gather_fusion.1, bf16[8,1024,512]{2,1,0:T(8,128)(2,1)} %gather_fusion), kind=kLoop, calls=%fused_computation.2 | loop fusion | flops 33554432 | bytes 33554432 | tf_op jit(solution)/shard_map/transpose | solution.py:11
  300.6 21.6 %copy.52 = bf16[2048,8,512]{0,2,1:T(8,128)(2,1)} copy(bf16[2048,8,512]{2,0,1:T(8,128)(2,1)} %maximum_bitcast_fusion) | data formatting | bytes 33554432 | tf_op jit(solution)/shard_map/transpose | solution.py:11
  322.2 10.6 %fusion.6 = bf16[128,2048]{0,1:T(8,128)(2,1)S(1)} fusion(bf16[2048,4096]{0,1:T(8,128)(2,1)} %bitcast.147, bf16[1,1,128,4096]{3,2,1,0:T(8,128)(2,1)} %all-gather.6.cloned.1.call-done, bf16[1,1,1,128,2048]{3,4,2,1,0:T(8,128)(2,1)S(1)} %copy-done.13), kind=kOutput, calls=%fused_computation.11 | convolution fusion | flops 2148270080 | bytes 18874368 | tf_op jit(solution)/shard_map/dot_general | solution.py:83
  354.0 6.1 reshape.244
  366.3 6.2 %reshape.246 = f32[16,128,255]{2,1,0:T(8,128)} reshape(f32[16,32640]{1,0:T(8,128)} %slice.298) | data formatting | bytes 4177920 | tf_op jit(solution)/shard_map/reshape | solution.py:59
  378.8 6.2 reshape.248
  391.4 6.2 reshape.250
  403.8 6.1 reshape.252
  416.1 6.2 reshape.254
  433.2 6.1 reshape.256
  443.7 6.2 reshape.258
  456.2 8.5 %fusion.5 = bf16[128,2048]{1,0:T(8,128)(2,1)S(1)} fusion(bf16[128,4096]{1,0:T(8,128)(2,1)} %all-gather.4.cloned.1.call-done, bf16[2048,4096]{0,1:T(8,128)(2,1)} %bitcast.148, bf16[1,2,1,128,2048]{4,3,2,1,0:T(8,128)(2,1)} %param.7), kind=kOutput, calls=%fused_computation.10 | convolution fusion | flops 2148270080 | bytes 18874368 | tf_op jit(solution)/shard_map/dot_general | solution.py:83
  482.0 6.2 %reshape.260 = f32[16,128,255]{2,1,0:T(8,128)} reshape(f32[16,32640]{1,0:T(8,128)} %slice.312) | data formatting | bytes 4177920 | tf_op jit(solution)/shard_map/reshape | solution.py:59
  494.4 6.1 reshape.262
  506.7 6.4 %reshape.264 = f32[16,128,255]{2,1,0:T(8,128)} reshape(f32[16,32640]{1,0:T(8,128)} %slice.316) | data formatting | bytes 4177920 | tf_op jit(solution)/shard_map/reshape | solution.py:59
  519.4 6.2 reshape.266
  531.8 6.2 reshape.268
  544.2 6.4 %reshape.270 = f32[16,128,255]{2,1,0:T(8,128)} reshape(f32[16,32640]{1,0:T(8,128)} %slice.322) | data formatting | bytes 4177920 | tf_op jit(solution)/shard_map/reshape | solution.py:59
  556.8 6.2 reshape.272
  566.3 4.6 reshape.274
  576.5 33.9 %reduce-scatter.4.cloned.1.call-done = f32[16,128]{1,0:T(8,128)} async-done(((f32[128,128]{1,0:T(8,128)}), f32[16,128]{1,0:T(8,128)}) %reduce-scatter.4.cloned.1.call-update) | async-done | bytes 8208
  (172 shorter events, 171.6 us)
Async XLA Ops:
  7.2 150.7 %copy-start.14 = (bf16[1,128,128]{2,1,0:T(8,128)(2,1)S(1)}, bf16[1,128,128]{2,1,0:T(8,128)(2,1)}, u32[]{:S(2)}) copy-start(bf16[1,128,128]{2,1,0:T(8,128)(2,1)} %param.11) | copy-start | bytes 98308
  7.2 315.1 %all-gather.6.cloned.1.call-start = ((), (), s32[]{:S(2)}) async-start(), calls=%async_computation.2 | async-start | bytes 1572864 | tf_op jit(solution)/shard_map/all_gather | solution.py:80
  7.2 51.8 %collective-permute-start = (bf16[2048,512]{1,0:T(8,128)(2,1)}, bf16[2048,512]{1,0:T(8,128)(2,1)S(1)}, u32[]{:S(2)}, u32[]{:S(2)}) collective-permute-start(bf16[2048,512]{1,0:T(8,128)(2,1)} %bitcast.208), channel_id=1, source_target_pairs={{0,2},{2,4},{4,6},{6,8},{8,10},{10,12},{12,14},{14,0},{1,3},{3,5},... | collective-permute-start | bytes 6291464 | tf_op jit(solution)/shard_map/ppermute | solution.py:21
  59.0 48.0 %collective-permute-start.1 = (bf16[2048,512]{1,0:T(8,128)(2,1)S(1)}, bf16[2048,512]{1,0:T(8,128)(2,1)S(1)}, u32[]{:S(2)}, u32[]{:S(2)}) collective-permute-start(bf16[2048,512]{1,0:T(8,128)(2,1)S(1)} %collective-permute-done), channel_id=1, source_target_pairs={{0,2},{2,4},{4,6},{6,8},{8,10},{10,12},{12,14},{14,0},{1,3},{3,5},... | collective-permute-start | bytes 6291464 | tf_op jit(solution)/shard_map/ppermute | solution.py:21
  59.0 49.3 %collective-permute-start.4 = (bf16[2048,512]{1,0:T(8,128)(2,1)}, bf16[2048,512]{1,0:T(8,128)(2,1)}, u32[]{:S(2)}, u32[]{:S(2)}) collective-permute-start(bf16[2048,512]{1,0:T(8,128)(2,1)} %bitcast.209), channel_id=1, source_target_pairs={{2,0},{4,2},{6,4},{8,6},{10,8},{12,10},{14,12},{0,14},{3,1},{5,3},... | collective-permute-start | bytes 6291464 | tf_op jit(solution)/shard_map/ppermute | solution.py:23
  107.0 1.3 copy-start.10
  108.3 47.2 %collective-permute-start.2 = (bf16[2048,512]{1,0:T(8,128)(2,1)S(1)}, bf16[2048,512]{1,0:T(8,128)(2,1)}, u32[]{:S(2)}, u32[]{:S(2)}) collective-permute-start(bf16[2048,512]{1,0:T(8,128)(2,1)S(1)} %collective-permute-done.1), channel_id=1, source_target_pairs={{0,2},{2,4},{4,6},{6,8},{8,10},{10,12},{12,14},{14,0},{1,3},{3,5},... | collective-permute-start | bytes 6291464 | tf_op jit(solution)/shard_map/ppermute | solution.py:21
  108.3 110.2 %collective-permute-start.5 = (bf16[2048,512]{1,0:T(8,128)(2,1)}, bf16[2048,512]{1,0:T(8,128)(2,1)}, u32[]{:S(2)}, u32[]{:S(2)}) collective-permute-start(bf16[2048,512]{1,0:T(8,128)(2,1)} %collective-permute-done.4), channel_id=1, source_target_pairs={{2,0},{4,2},{6,4},{8,6},{10,8},{12,10},{14,12},{0,14},{3,1},{5,3},... | collective-permute-start | bytes 6291464 | tf_op jit(solution)/shard_map/ppermute | solution.py:23
  155.5 66.7 %collective-permute-start.3 = (bf16[2048,512]{1,0:T(8,128)(2,1)}, bf16[2048,512]{1,0:T(8,128)(2,1)}, u32[]{:S(2)}, u32[]{:S(2)}) collective-permute-start(bf16[2048,512]{1,0:T(8,128)(2,1)} %collective-permute-done.2), channel_id=1, source_target_pairs={{0,2},{2,4},{4,6},{6,8},{8,10},{10,12},{12,14},{14,0},{1,3},{3,5},... | collective-permute-start | bytes 6291464 | tf_op jit(solution)/shard_map/ppermute | solution.py:21
  155.6 300.6 %all-gather.4.cloned.1.call-start = ((), (), s32[]{:S(2)}) async-start(), calls=%async_computation.1 | async-start | bytes 1572864 | tf_op jit(solution)/shard_map/all_gather | solution.py:80
  181.3 29.6 %copy-start.1 = (bf16[1,2,1,128,2048]{4,3,2,1,0:T(8,128)(2,1)S(1)}, bf16[1,2,1,128,2048]{4,3,2,1,0:T(8,128)(2,1)}, u32[]{:S(2)}) copy-start(bf16[1,2,1,128,2048]{4,3,2,1,0:T(8,128)(2,1)} %param.8) | copy-start | bytes 3145732
  218.6 46.2 %collective-permute-start.6 = (bf16[2048,512]{1,0:T(8,128)(2,1)}, bf16[2048,512]{1,0:T(8,128)(2,1)S(1)}, u32[]{:S(2)}, u32[]{:S(2)}) collective-permute-start(bf16[2048,512]{1,0:T(8,128)(2,1)} %collective-permute-done.5), channel_id=1, source_target_pairs={{2,0},{4,2},{6,4},{8,6},{10,8},{12,10},{14,12},{0,14},{3,1},{5,3},... | collective-permute-start | bytes 6291464 | tf_op jit(solution)/shard_map/ppermute | solution.py:23
  224.0 2.2 copy-start.11
  226.4 1.6 copy-start.9
  300.6 21.6 %copy-start.13 = (bf16[1,1,1,128,2048]{3,4,2,1,0:T(8,128)(2,1)S(1)}, bf16[1,1,1,128,2048]{3,4,2,1,0:T(8,128)(2,1)}, u32[]{:S(2)}) copy-start(bf16[1,1,1,128,2048]{3,4,2,1,0:T(8,128)(2,1)} %copy.63) | copy-start | bytes 1572868
  332.9 10.1 %slice-start = ((s8[8388608]{0:T(1024)(128)(4,1)}), s8[4194304]{0:T(1024)(128)(4,1)S(1)}, s32[]{:S(2)}) async-start(s8[8388608]{0:T(1024)(128)(4,1)} %bitcast.149), calls=%async_computation.4 | async-start | bytes 8388608
  338.0 5.0 slice-start.1
  345.3 1.3 copy-start.4
  346.6 4.6 copy-start
  349.2 78.5 %collective-permute-start.7 = (bf16[128,2048]{1,0:T(8,128)(2,1)}, bf16[128,2048]{1,0:T(8,128)(2,1)S(1)}, u32[]{:S(2)}, u32[]{:S(2)}) collective-permute-start(bf16[128,2048]{1,0:T(8,128)(2,1)} %fusion.10), channel_id=1, source_target_pairs={{16,0},{32,16},{48,32},{64,48},{80,64},{96,80},{112,96},{128,112},... | collective-permute-start | bytes 1572872 | tf_op jit(solution)/shard_map/ppermute | solution.py:33
  427.6 0.8 copy-start.8
  428.4 182.0 %reduce-scatter.4.cloned.1.call-start = ((), (), s32[]{:S(2)}) async-start(), calls=%async_computation.3 | async-start | bytes 73728
  449.9 5.3 copy-start.2
  449.9 5.3 copy-start.5
  451.2 4.0 copy-start.6
  465.3 10.7 %slice-start.2 = ((s8[8388608]{0:T(1024)(128)(4,1)}), s8[4194304]{0:T(1024)(128)(4,1)S(1)}, s32[]{:S(2)}) async-start(s8[8388608]{0:T(1024)(128)(4,1)} %bitcast.151), calls=%async_computation.6 | async-start | bytes 8388608
  470.4 5.6 slice-start.3
  566.3 7.5 %copy-start.7 = (f32[128,16,128]{2,1,0:T(8,128)S(1)}, f32[128,16,128]{2,1,0:T(8,128)}, u32[]{:S(2)}) copy-start(f32[128,16,128]{2,1,0:T(8,128)} %fusion) | copy-start | bytes 3145732
  570.9 3.2 copy-start.3
  574.1 1.3 copy-start.12
Sparse Core Ops, SparseCore 0:
  155.7 26.9 all-gather.5
  428.6 27.1 all-gather.3
  573.9 36.5 reduce-scatter.3
